TPU v7x, 128 devices: a whole 4x4x4 slice. The times are simulated.
128 devices in a mesh: fibre: 16 (over x, z_hi, core), tm: 8 (over y, z_lo).
Axes of the slice: x: 4, y: 4, z: 4 (z_hi: 2, z_lo: 2; z = z_hi * 2 + z_lo), core: 2. Of those that a mesh axis runs over, the one named last changes fastest.
Arguments:
- samples: bfloat16 [65536, 8192], P('tm', 'fibre'), may hold values from -6 to 6
- filter_taps: float32 [16, 512], replicated, may hold values from -1.5 to 1.5
- steering: bfloat16 [128, 2, 128, 1024], P('tm'), may hold values from -0.1875 to 0.1875
Outputs:
- beam_power: float32 [32, 128, 128, 128], P('fibre', 'tm')
All inputs are finite; a program needn't handle non-finite values.
Results may differ from a plain program's by a relative error of at most 0.0052.
Values may be sent and summed in bfloat16 or wider, within the bound.
A program may use at most 704 MiB of HBM per device.

v0:
```python
import math

import jax
import jax.numpy as jnp
from jax import lax
from jax.sharding import PartitionSpec as P

NFFT = 512
TAPS = 16
KB = 128
KLO = 64
APER = 1024
STRIDE = 256
HALO = 384


def from_behind(value, axis, steps):
    count = lax.axis_size(axis)
    initial, last = (max(0, -steps), min(count, count - steps))
    return lax.ppermute(value, axis, [(source, source + steps) for source in range(initial, last)])


def with_halo(block, sides, width):
    for axis, dim in sides:
        count = lax.axis_size(axis)
        forward = [(i, i + 1) for i in range(count - 1)]
        backward = [(target, source) for source, target in forward]
        low = lax.ppermute(
            lax.slice_in_dim(block, block.shape[dim] - width, None, axis=dim), axis, forward
        )
        high = lax.ppermute(lax.slice_in_dim(block, 0, width, axis=dim), axis, backward)
        block = jnp.concatenate([low, block, high], axis=dim)
    return block


def dft_table():
    sample_index = jnp.arange(NFFT, dtype=jnp.int32)
    bin_index = jnp.arange(KB, dtype=jnp.int32) + KLO
    phases = (bin_index[:, None] * sample_index[None, :] % NFFT).astype(jnp.float32) * (
        2.0 * math.pi / NFFT
    )
    fourier = jnp.concatenate([jnp.cos(phases), -jnp.sin(phases)], 0) / math.sqrt(NFFT)
    return fourier.astype(jnp.bfloat16)


def filterbank(longer, filter_taps, fourier):
    channels = longer.shape[1]
    count_frames = longer.shape[0] // NFFT - (TAPS - 1)
    framed = longer.reshape(count_frames + TAPS - 1, NFFT, channels)
    terms = [
        filter_taps[tap_index][None, :, None]
        * framed[TAPS - 1 - tap_index : TAPS - 1 - tap_index + count_frames].astype(jnp.float32)
        for tap_index in range(TAPS)
    ]
    filtered = terms[0]
    for extra in terms[1:]:
        filtered = filtered + extra
    filtered = filtered.astype(jnp.bfloat16)
    spectra = jnp.einsum("kn,fnc->fkc", fourier, filtered, preferred_element_type=jnp.float32)
    return spectra.astype(jnp.bfloat16).reshape(count_frames, 2, KB, channels)


def beam_power(gathered, steering, offset):
    window = gathered[:, :, :, offset : offset + APER]
    products = jnp.einsum("fpkc,kqsc->kfpqs", window, steering, preferred_element_type=jnp.float32)
    real_part = products[:, :, 0, 0, :] - products[:, :, 1, 1, :]
    imag_part = products[:, :, 1, 0, :] + products[:, :, 0, 1, :]
    return real_part * real_part + imag_part * imag_part


def body(samples, filter_taps, steering):
    fourier = dft_table()
    history_length = (TAPS - 1) * NFFT
    history_rows = from_behind(samples[samples.shape[0] - history_length :], "tm", 1)
    longer = jnp.concatenate([history_rows, samples], 0)
    spectra = filterbank(longer, filter_taps, fourier)
    gathered = lax.all_to_all(spectra, "tm", split_axis=2, concat_axis=0, tiled=True)
    gathered = with_halo(gathered, (("fibre", 3),), HALO)
    aperture_count = (gathered.shape[3] - 2 * HALO) // STRIDE
    beam_list = [
        beam_power(gathered, steering, aperture * STRIDE) for aperture in range(aperture_count)
    ]
    return jnp.stack(beam_list, 0)


def solution(mesh):
    in_specs = (P("tm", "fibre"), P(), P("tm", None, None, None))
    out_specs = P("fibre", "tm", None, None)
    return jax.shard_map(body, mesh=mesh, in_specs=in_specs, out_specs=out_specs, check_vma=False)
```

profile of v0, /device:TPU:1, one launch (start us, length us, event | category | flops | bytes accessed | tf_op | source)
XLA Modules:
  0.0 494.0 jit_solution(4808834405614839922)
XLA Ops:
  0.0 0.0 copy-start
  0.0 6.8 %slice.151 = bf16[7680,512]{1,0:T(8,128)(2,1)} slice(bf16[8192,512]{1,0:T(8,128)(2,1)} %param.3), slice={[512:8192], [0:512]} | slice | bytes 15728640 | tf_op jit(solution)/shard_map/slice | solution.py:74
  6.8 4.9 collective-permute-start
  11.7 0.0 copy-done
  11.7 1.1 fusion.44
  12.8 166.5 %collective-permute-done = bf16[7680,512]{1,0:T(8,128)(2,1)S(1)} collective-permute-done((bf16[7680,512]{1,0:T(8,128)(2,1)}, bf16[7680,512]{1,0:T(8,128)(2,1)S(1)}, u32[]{:S(2)}, u32[]{:S(2)}) %collective-permute-start) | collective-permute-done | bytes 7864352 | tf_op jit(solution)/shard_map/ppermute | solution.py:20
  179.4 3.6 constant_dynamic-update-slice_fusion.1
  182.9 7.2 %constant_dynamic-update-slice_fusion = bf16[15872,512]{1,0:T(8,128)(2,1)} fusion(bf16[15872,512]{1,0:T(8,128)(2,1)} %constant_dynamic-update-slice_fusion.1, bf16[8192,512]{1,0:T(8,128)(2,1)} %param.3), kind=kLoop, calls=%fused_computation.70 | loop fusion | bytes 16777216 | tf_op jit(solution)/shard_map/concatenate | solution.py:75
  190.1 81.6 %fusion.47 = (bf16[8192,512]{1,0:T(8,128)(2,1)}, bf16[8192,512]{1,0:T(8,128)(2,1)}, bf16[8192,512]{1,0:T(8,128)(2,1)}, bf16[8192,512]{1,0:T(8,128)(2,1)}, bf16[8...) fusion(bf16[15872,512]{1,0:T(8,128)(2,1)} %constant_dynamic-upd, ...), kind=kLoop, calls=%fused_computation.75 | loop fusion | bytes 251658240 | tf_op jit(solution)/shard_map/slice | solution.py:52
  271.7 51.6 %fusion.23 = bf16[16,512,256]{1,2,0:T(8,128)(2,1)} fusion(bf16[16,512,512]{2,1,0:T(8,128)(2,1)} %bitcast.86, bf16[16,512,512]{2,1,0:T(8,128)(2,1)} %bitcast.87, bf16[16,512,512]{2,1,0:T(8,128)(2,1)} %bitcast.88, bf16[16,512,512]{2,1,0:T(8,128)(2,1)} %bitcast.89, bf16[16,512,512]{2,1,0:T(8,128)(2,1)} %bitcast.90, bf16[16,512,512]{2,1,0:T(8,128)(2,1)} %bitcast.91, ...), kind=kOutput, calls=%fused_computation.41 | convolution fusion | flops 2351300608 | bytes 138969088 | tf_op jit(solution)/shard_map/kn,fnc->fkc/dot_general | solution.py:59
  323.3 6.5 %copy.9 = bf16[16,2,128,512]{3,1,0,2:T(2,128)(2,1)S(1)} copy(bf16[16,2,128,512]{3,2,1,0:T(8,128)(2,1)} %bitcast.100) | data formatting | bytes 8388608 | tf_op jit(solution)/shard_map/reshape | solution.py:60
  329.8 52.5 %all_to_all.18 = bf16[16,2,128,512]{3,1,0,2:T(2,128)(2,1)S(1)} all-to-all(bf16[16,2,128,512]{3,1,0,2:T(2,128)(2,1)S(1)} %copy.9), channel_id=1, replica_groups=mesh['fibre'=16,'tm'=8] {'tm'}, dimensions={2} | all-to-all | bytes 8388608 | tf_op jit(solution)/shard_map/all_to_all | solution.py:77
  382.3 1.0 copy.10
  383.3 1.0 fusion.48
  384.3 5.2 %collective-permute-start.2 = (bf16[128,2,16,384]{3,0,1,2:T(8,128)(2,1)S(1)}, bf16[128,2,16,384]{3,0,1,2:T(8,128)(2,1)S(1)}, u32[]{:S(2)}, u32[]{:S(2)}) collective-permute-start(bf16[128,2,16,384]{3,0,1,2:T(8,128)(2,1)S(1)} %get-tuple-element.21), channel_id=1, source_target_pairs={{8,0},{16,8},{24,16},{32,24},{40,32},{48,40},{56,48},{64,56},{72,6... | collective-permute-start | bytes 9437192 | tf_op jit(solution)/shard_map/ppermute | solution.py:31
  389.6 5.1 %collective-permute-start.1 = (bf16[128,2,16,384]{3,0,1,2:T(8,128)(2,1)S(1)}, bf16[128,2,16,384]{3,0,1,2:T(8,128)(2,1)S(1)}, u32[]{:S(2)}, u32[]{:S(2)}) collective-permute-start(bf16[128,2,16,384]{3,0,1,2:T(8,128)(2,1)S(1)} %get-tuple-element.20), channel_id=1, source_target_pairs={{0,8},{8,16},{16,24},{24,32},{32,40},{40,48},{48,56},{56,64},{64,7... | collective-permute-start | bytes 9437192 | tf_op jit(solution)/shard_map/ppermute | solution.py:28
  394.7 33.0 %collective-permute-done.2 = bf16[128,2,16,384]{3,0,1,2:T(8,128)(2,1)S(1)} collective-permute-done((bf16[128,2,16,384]{3,0,1,2:T(8,128)(2,1)S(1)}, bf16[128,2,16,384]{3,0,1,2:T(8,128)(2,1)S(1)}, u32[]{:S(2)}, u32[]{:S(2)}) %collective-permute-start.2) | collective-permute-done | bytes 3145760 | tf_op jit(solution)/shard_map/ppermute | solution.py:31
  427.7 31.2 %collective-permute-done.1 = bf16[128,2,16,384]{3,0,1,2:T(8,128)(2,1)S(1)} collective-permute-done((bf16[128,2,16,384]{3,0,1,2:T(8,128)(2,1)S(1)}, bf16[128,2,16,384]{3,0,1,2:T(8,128)(2,1)S(1)}, u32[]{:S(2)}, u32[]{:S(2)}) %collective-permute-start.1) | collective-permute-done | bytes 3145760 | tf_op jit(solution)/shard_map/ppermute | solution.py:28
  458.9 8.3 %pad_maximum_fusion = bf16[128,2,16,1280]{3,0,1,2:T(8,128)(2,1)} fusion(bf16[128,2,16,384]{3,0,1,2:T(8,128)(2,1)S(1)} %collective-permute-done.2, bf16[128,2,16,512]{3,0,1,2:T(8,128)(2,1)S(1)} %bitcast.82, bf16[128,2,16,384]{3,0,1,2:T(8,128)(2,1)S(1)} %collective-permute-done.1), kind=kLoop, calls=%fused_computation.32 | loop fusion | flops 31457280 | bytes 20971520 | tf_op jit(solution)/shard_map/concatenate | solution.py:32
  467.3 10.2 %fusion.18 = f32[16,128,2,2,128]{4,1,0,3,2:T(8,128)} fusion(bf16[128,2,16,1280]{3,0,1,2:T(8,128)(2,1)} %pad_maximum_fusion, bf16[16,2,128,1024]{3,2,1,0:T(8,128)(2,1)} %param.5), kind=kOutput, calls=%fused_computation.37 | convolution fusion | flops 2147483648 | bytes 20971520 | tf_op jit(solution)/shard_map/fpkc,kqsc->kfpqs/dot_general | solution.py:65
  477.5 10.1 %fusion.16 = f32[16,128,2,2,128]{4,1,3,2,0:T(8,128)} fusion(bf16[128,2,16,1280]{3,0,1,2:T(8,128)(2,1)} %pad_maximum_fusion, bf16[16,2,128,1024]{3,2,1,0:T(8,128)(2,1)} %param.5), kind=kOutput, calls=%fused_computation.35 | convolution fusion | flops 2147483648 | bytes 20971520 | tf_op jit(solution)/shard_map/fpkc,kqsc->kfpqs/dot_general | solution.py:65
  487.6 2.5 fusion.28
  490.1 2.5 fusion.32
  492.6 1.5 pad_maximum_fusion.1
  (2 shorter events, 0.0 us)
Async XLA Ops:
  0.0 11.7 %copy-start = (f32[16,512]{1,0:T(8,128)S(1)}, f32[16,512]{1,0:T(8,128)}, u32[]{:S(2)}) copy-start(f32[16,512]{1,0:T(8,128)} %param.4) | copy-start | bytes 98308
  6.8 172.6 %collective-permute-start = (bf16[7680,512]{1,0:T(8,128)(2,1)}, bf16[7680,512]{1,0:T(8,128)(2,1)S(1)}, u32[]{:S(2)}, u32[]{:S(2)}) collective-permute-start(bf16[7680,512]{1,0:T(8,128)(2,1)} %slice.151), channel_id=1, source_target_pairs={{0,1},{1,2},{2,3},{3,4},{4,5},{5,6},{6,7},{8,9},{9,10},{10,11},{11... | collective-permute-start | bytes 23592968 | tf_op jit(solution)/shard_map/ppermute | solution.py:20
  384.3 43.3 %collective-permute-start.2 = (bf16[128,2,16,384]{3,0,1,2:T(8,128)(2,1)S(1)}, bf16[128,2,16,384]{3,0,1,2:T(8,128)(2,1)S(1)}, u32[]{:S(2)}, u32[]{:S(2)}) collective-permute-start(bf16[128,2,16,384]{3,0,1,2:T(8,128)(2,1)S(1)} %get-tuple-element.21), channel_id=1, source_target_pairs={{8,0},{16,8},{24,16},{32,24},{40,32},{48,40},{56,48},{64,56},{72,6... | collective-permute-start | bytes 9437192 | tf_op jit(solution)/shard_map/ppermute | solution.py:31
  389.6 69.4 %collective-permute-start.1 = (bf16[128,2,16,384]{3,0,1,2:T(8,128)(2,1)S(1)}, bf16[128,2,16,384]{3,0,1,2:T(8,128)(2,1)S(1)}, u32[]{:S(2)}, u32[]{:S(2)}) collective-permute-start(bf16[128,2,16,384]{3,0,1,2:T(8,128)(2,1)S(1)} %get-tuple-element.20), channel_id=1, source_target_pairs={{0,8},{8,16},{16,24},{24,32},{32,40},{40,48},{48,56},{56,64},{64,7... | collective-permute-start | bytes 9437192 | tf_op jit(solution)/shard_map/ppermute | solution.py:28
where the time goes:
time: 496 us; the launch traced here: 494 us
  waiting for transfers between devices  231 us (47%)
  local copies, waits for them, and re-layouts  108 us (22%)
  matrix products  71.9 us (14%)
  blocking collectives  52.5 us (11%)
  other arithmetic  15.9 us (3%)
  starting transfers between devices  15.2 us (3%)
    ppermute x1, waiting for transfers between devices, from_behind(): lax.ppermute(value, axis, [(source, source + steps) for source in range(i...  167 us
    slice x1, local copies, waits for them, and re-layouts, filterbank(): framed[TAPS - 1 - tap_index:TAPS - 1 - tap_index + count_frames]  81.6 us
    all_to_all x1, blocking collectives, body(): lax.all_to_all(spectra, 'tm', split_axis=2, concat_axis=0, tiled=True)  52.5 us
    dot_general x1, matrix products, filterbank(): jnp.einsum('kn,fnc->fkc', fourier, filtered, preferred_element_type=jnp.f...  51.6 us
    ppermute x1, waiting for transfers between devices, with_halo(): lax.ppermute(lax.slice_in_dim(block, 0, width, axis=dim), axis, backward)  33 us
    ppermute x1, waiting for transfers between devices, with_halo(): lax.ppermute(lax.slice_in_dim(block, block.shape[dim] - width, None, axis...  31.2 us
    dot_general x2, matrix products, beam_power(): jnp.einsum('fpkc,kqsc->kfpqs', window, steering, preferred_element_type=j...  20.3 us
  transfers between devices with their start and end apart: 3, of which 3 were waited for; matrix products, arithmetic and copies ran while one was open for 0% of the time, Pallas kernels for 0%

commit v1 on v0

v1 whole, which is shorter than its diff:
```python
import math

import jax
import jax.numpy as jnp
from jax import lax
from jax.experimental import pallas as pl
from jax.experimental.pallas import tpu as pltpu
from jax.sharding import PartitionSpec as P

NFFT = 512
TAPS = 16
KB = 128
KLO = 64
APER = 1024
FRAMES = 128
SLOW = 128

BLOCK = 16
SPAN = 31
CHUNK = 128
CHUNKS = 4
TM = 8
BINS = 16

MESH = pl.DeviceIdType.MESH
f32 = jnp.float32
bf16 = jnp.bfloat16

OFFSETS = ((0, 1), (1, 0), (3, 0), (2, 1), (1, 1), (2, 0), (3, 1))


def dft_table():
    sample_index = jnp.arange(NFFT, dtype=jnp.int32)
    bin_index = jnp.arange(KB, dtype=jnp.int32) + KLO
    phases = (bin_index[:, None] * sample_index[None, :] % NFFT).astype(f32) * (
        2.0 * math.pi / NFFT
    )
    fourier = jnp.stack([jnp.cos(phases), -jnp.sin(phases)], 0) / math.sqrt(NFFT)
    fourier = fourier.reshape(2, TM, BINS, NFFT).transpose(1, 0, 2, 3)
    return fourier.reshape(2 * KB, NFFT).astype(bf16)


def shifted(tm, dy, flip, sign):
    y, lo = tm // 2, tm % 2
    y = lax.rem(y + (dy if sign > 0 else 4 - dy), 4)
    return 2 * y + (1 - lo if flip else lo)


def kernel(
    x_ref, taps_ref, fourier_ref, steer_ref, out_ref,
    xb, wide, filt, send, recv, steer, spec, off_out, off_in, on_out, on_in,
    x_sem, steer_sem, own_sem, send_sem, recv_sem, off_ssem, off_rsem, on_ssem, on_rsem,
):
    tm = lax.axis_index("tm")
    fibre = lax.axis_index("fibre")
    core = fibre % 2
    count = 16
    partner = fibre + 1 - 2 * core
    outer = lax.rem(fibre + count - 1 + 2 * core, count)

    def there(tm_index, fibre_index):
        return {"fibre": fibre_index, "tm": tm_index}

    def chunk_of(step):
        return jnp.where(core == 0, step, CHUNKS - 1 - step)

    def x_copy(step):
        column = pl.multiple_of(chunk_of(step) * CHUNK, CHUNK)
        slot = step % 2
        return pltpu.make_async_copy(
            x_ref.at[:, :, pl.ds(column, CHUNK)], xb.at[slot], x_sem.at[slot]
        )

    steer_copy = pltpu.make_async_copy(steer_ref, steer, steer_sem)

    x_copy(0).start()
    steer_copy.start()

    barrier = pltpu.get_barrier_semaphore()
    for dy, flip in OFFSETS:
        pl.semaphore_signal(
            barrier, inc=1, device_id=there(shifted(tm, dy, flip, 1), fibre), device_id_type=MESH
        )
    for other in (partner, outer):
        pl.semaphore_signal(barrier, inc=1, device_id=there(tm, other), device_id_type=MESH)

    wide[...] = jnp.broadcast_to(taps_ref[...][:, :, None], (TAPS, NFFT, CHUNK))
    filt[:, SPAN * CHUNK :] = jnp.zeros((NFFT, CHUNK), bf16)
    recv[:, :, SPAN:] = jnp.zeros((CHUNKS, TM, 1, 2 * BINS, CHUNK), bf16)

    def to_peer(step, index):
        dy, flip = OFFSETS[index]
        target = shifted(tm, dy, flip, 1)
        return pltpu.make_async_remote_copy(
            src_ref=send.at[step, target, pl.ds(0, SPAN)],
            dst_ref=recv.at[step, tm, pl.ds(0, SPAN)],
            send_sem=send_sem.at[step, index],
            recv_sem=recv_sem.at[step, index],
            device_id=there(target, fibre),
            device_id_type=MESH,
        )

    def from_peer(step, index):
        dy, flip = OFFSETS[index]
        source = shifted(tm, dy, flip, -1)
        return pltpu.make_async_remote_copy(
            src_ref=send.at[step, source, pl.ds(0, SPAN)],
            dst_ref=recv.at[step, source, pl.ds(0, SPAN)],
            send_sem=send_sem.at[step, index],
            recv_sem=recv_sem.at[step, index],
            device_id=there(source, fibre),
            device_id_type=MESH,
        )

    def own_copy(step):
        return pltpu.make_async_copy(
            send.at[step, tm, pl.ds(0, SPAN)], recv.at[step, tm, pl.ds(0, SPAN)], own_sem.at[step]
        )

    def halo(out, landing, ssem, rsem, aperture, other):
        return pltpu.make_async_remote_copy(
            src_ref=out.at[aperture],
            dst_ref=landing.at[aperture],
            send_sem=ssem.at[aperture],
            recv_sem=rsem.at[aperture],
            device_id=there(tm, other),
            device_id_type=MESH,
        )

    def off_copy(aperture):
        return halo(off_out, off_in, off_ssem, off_rsem, aperture, outer)

    def on_copy(aperture):
        return halo(on_out, on_in, on_ssem, on_rsem, aperture, partner)

    def produce(step, carry):
        slot = step % 2
        x_copy(step).wait()

        @pl.when(step < CHUNKS - 1)
        def _():
            x_copy(step + 1).start()

        def filter_rows(index, carry):
            rows = pl.ds(pl.multiple_of(index * 16, 16), 16)
            xs = [xb[slot, g, rows, :].astype(f32) for g in range(BLOCK)]
            ts = [wide[t, rows, :] for t in range(TAPS)]
            for frame in range(SPAN):
                first, last = max(0, frame - BLOCK + 1), min(TAPS - 1, frame)
                total = ts[first] * xs[frame - first]
                for t in range(first + 1, last + 1):
                    total = total + ts[t] * xs[frame - t]
                filt[rows, frame * CHUNK : (frame + 1) * CHUNK] = total.astype(bf16)
            return carry

        lax.fori_loop(0, NFFT // 16, filter_rows, 0)

        def transform(pair, carry):
            columns = pl.ds(pl.multiple_of(pair * 2 * CHUNK, 2 * CHUNK), 2 * CHUNK)
            values = jnp.dot(
                fourier_ref[...], filt[:, columns], preferred_element_type=f32
            ).astype(bf16)
            for half in range(2):
                for d in range(TM):
                    send[step, d, pair * 2 + half] = values[
                        d * 2 * BINS : (d + 1) * 2 * BINS, half * CHUNK : (half + 1) * CHUNK
                    ]
            return carry

        lax.fori_loop(0, (SPAN + 1) // 2, transform, 0)

        @pl.when(step == 0)
        def _():
            pl.semaphore_wait(barrier, len(OFFSETS) + 2)

        for index in range(len(OFFSETS)):
            to_peer(step, index).start()
        own_copy(step).start()
        return carry

    lax.fori_loop(0, CHUNKS, produce, 0)

    def combine(step):
        for index in range(len(OFFSETS)):
            from_peer(step, index).wait_recv()
        own_copy(step).wait()
        columns = pl.ds(pl.multiple_of(chunk_of(step) * CHUNK, CHUNK), CHUNK)

        def block(i, carry):
            before = jnp.maximum(i - 1, 0)
            late = recv[step, before, pl.ds(BLOCK, BLOCK)].astype(f32)
            total = recv[step, i, pl.ds(0, BLOCK)].astype(f32) + jnp.where(i > 0, late, 0.0)
            turned = jnp.transpose(total, (1, 0, 2)).astype(bf16)
            for p in range(2):
                rows = pl.ds(pl.multiple_of(p * FRAMES + i * BLOCK, BLOCK), BLOCK)
                spec[:, rows, columns] = turned[p * BINS : (p + 1) * BINS]
            return carry

        lax.fori_loop(0, TM, block, 0)

    def product(k, u, width, m):
        if not isinstance(u, int):
            u, m = pl.multiple_of(u, CHUNK), pl.multiple_of(m, CHUNK)
        left = spec[k, :, pl.ds(u, width)]
        right = steer[k, :, pl.ds(m, width)]
        values = lax.dot_general(
            left, right, (((1,), (1,)), ((), ())), preferred_element_type=f32
        )
        real = values[:FRAMES, :SLOW] - values[FRAMES:, SLOW:]
        imag = values[FRAMES:, :SLOW] + values[:FRAMES, SLOW:]
        return real, imag

    def near(to_left, width):
        u = jnp.where(to_left, 0, 512 - width)
        m = jnp.where(to_left, APER - width, 0)
        return u, m

    def side(out, aperture, to_left, width):
        u, m = near(to_left, width)

        def one(k, carry):
            real, imag = product(k, u, width, m)
            out[aperture, k, 0] = real.astype(bf16)
            out[aperture, k, 1] = imag.astype(bf16)
            return carry

        lax.fori_loop(0, BINS, one, 0)

    combine(0)
    steer_copy.wait()
    side(off_out, core, core == 0, 128)
    off_copy(core).start()
    combine(1)
    combine(2)
    side(off_out, 1 - core, core == 0, 384)
    off_copy(1 - core).start()
    combine(3)
    side(on_out, 1 - core, core == 1, 128)
    on_copy(1 - core).start()
    side(on_out, core, core == 1, 384)
    on_copy(core).start()

    def own(k, carry):
        for aperture in range(2):
            real, imag = product(k, 0, 512, 384 - 256 * aperture)
            wide[k, pl.ds(aperture * 256, 128)] = real
            wide[k, pl.ds(aperture * 256 + 128, 128)] = imag
        return carry

    lax.fori_loop(0, BINS, own, 0)

    for aperture in range(2):
        on_copy(aperture).wait()
        off_copy(aperture).wait()
    inside = jnp.logical_and(
        jnp.logical_or(fibre > 0, core == 1), jnp.logical_or(fibre < count - 1, core == 0)
    )

    def finish(k, carry):
        for aperture in range(2):
            parts = []
            for part in range(2):
                total = wide[k, pl.ds(aperture * 256 + part * 128, 128)]
                total = total + on_in[aperture, k, part].astype(f32)
                total = total + jnp.where(inside, off_in[aperture, k, part].astype(f32), 0.0)
                parts.append(total)
            out_ref[aperture, k] = parts[0] * parts[0] + parts[1] * parts[1]
        return carry

    lax.fori_loop(0, BINS, finish, 0)

    def drain(step, carry):
        for index in range(len(OFFSETS)):
            to_peer(step, index).wait_send()
        return carry

    lax.fori_loop(0, CHUNKS, drain, 0)


def body(samples, filter_taps, steering):
    peers = len(OFFSETS)
    vmem = pl.BlockSpec(memory_space=pltpu.VMEM)
    hbm = pl.BlockSpec(memory_space=pl.ANY)
    dma = pltpu.SemaphoreType.DMA
    return pl.pallas_call(
        kernel,
        out_shape=jax.ShapeDtypeStruct((2, BINS, FRAMES, SLOW), f32),
        in_specs=[hbm, vmem, vmem, hbm],
        out_specs=vmem,
        scratch_shapes=[
            pltpu.VMEM((2, BLOCK, NFFT, CHUNK), bf16),
            pltpu.VMEM((TAPS, NFFT, CHUNK), f32),
            pltpu.VMEM((NFFT, (SPAN + 1) * CHUNK), bf16),
            pltpu.VMEM((CHUNKS, TM, SPAN + 1, 2 * BINS, CHUNK), bf16),
            pltpu.VMEM((CHUNKS, TM, SPAN + 1, 2 * BINS, CHUNK), bf16),
            pltpu.VMEM((BINS, 2 * SLOW, APER), bf16),
            pltpu.VMEM((BINS, 2 * FRAMES, CHUNKS * CHUNK), bf16),
            pltpu.VMEM((2, BINS, 2, FRAMES, SLOW), bf16),
            pltpu.VMEM((2, BINS, 2, FRAMES, SLOW), bf16),
            pltpu.VMEM((2, BINS, 2, FRAMES, SLOW), bf16),
            pltpu.VMEM((2, BINS, 2, FRAMES, SLOW), bf16),
            dma((2,)),
            dma,
            dma((CHUNKS,)),
            dma((CHUNKS, peers)),
            dma((CHUNKS, peers)),
            dma((2,)),
            dma((2,)),
            dma((2,)),
            dma((2,)),
        ],
        compiler_params=pltpu.CompilerParams(
            collective_id=0, has_side_effects=True, vmem_limit_bytes=60 * 2**20
        ),
        cost_estimate=pl.CostEstimate(
            flops=13 * 10**9, bytes_accessed=20 * 2**20, transcendentals=0
        ),
    )(
        samples.reshape(BLOCK, NFFT, samples.shape[1]),
        filter_taps,
        dft_table(),
        steering.reshape(BINS, 2 * SLOW, APER),
    )


def solution(mesh):
    in_specs = (P("tm", "fibre"), P(), P("tm", None, None, None))
    out_specs = P("fibre", "tm", None, None)
    return jax.shard_map(body, mesh=mesh, in_specs=in_specs, out_specs=out_specs, check_vma=False)
```

time: 496 us -> 161 us (0.32)
  waiting for transfers between devices: 231 us -> 0 us
  Pallas kernels: 0 us -> 156 us
  local copies, waits for them, and re-layouts: 108 us -> 3.14 us
  matrix products: 71.9 us -> 0 us
  blocking collectives: 52.5 us -> 0 us
  starting transfers between devices: 15.2 us -> 0 us
  other arithmetic: 15.9 us -> 1.86 us
    ppermute x3 -> x0, waiting for transfers between devices: 231 us -> none  [the longest x1 167 us: from_behind(): lax.ppermute(value, axis, [(source, source + steps) for source in range(i...]
    pallas_call x0 -> x1, Pallas kernels: none -> 156 us  [body(): pl.pallas_call(kernel, out_shape=jax.ShapeDtypeStruct((2, BINS, FRAMES, S...]
    slice x4 -> x0, local copies, waits for them, and re-layouts: 89.4 us -> none  [the longest x1 81.6 us: filterbank(): framed[TAPS - 1 - tap_index:TAPS - 1 - tap_index + count_frames]]
    dot_general x3 -> x0, matrix products: 71.9 us -> none  [the longest x1 51.6 us: filterbank(): jnp.einsum('kn,fnc->fkc', fourier, filtered, preferred_element_type=jnp.f...]
    all_to_all x1 -> x0, blocking collectives: 52.5 us -> none  [body(): lax.all_to_all(spectra, 'tm', split_axis=2, concat_axis=0, tiled=True)]
    ppermute x3 -> x0, starting transfers between devices: 15.2 us -> none  [the longest x1 5.21 us: with_halo(): lax.ppermute(lax.slice_in_dim(block, 0, width, axis=dim), axis, backward)]
    concatenate x1 -> x0, other arithmetic: 8.33 us -> none  [with_halo(): block = jnp.concatenate([low, block, high], axis=dim)]
    concatenate x1 -> x0, local copies, waits for them, and re-layouts: 7.17 us -> none  [body(): longer = jnp.concatenate([history_rows, samples], 0)]
  transfers between devices with their start and end apart: 3 -> 0, of which waited for: 3 -> 0; matrix products, arithmetic and copies ran while one was open for 0% -> 0% of each run, Pallas kernels for 0% -> 0%
where the time goes in v1:
time: 161 us
  Pallas kernels  156 us (97%)
  local copies, waits for them, and re-layouts  3.14 us (2%)
  other arithmetic  1.86 us (1%)
    pallas_call x1, Pallas kernels, body(): pl.pallas_call(kernel, out_shape=jax.ShapeDtypeStruct((2, BINS, FRAMES, S...  156 us

profile of v1, /device:TPU:1, one launch (start us, length us, event | category | flops | bytes accessed | tf_op | source)
XLA Modules:
  0.0 161.3 jit_solution(12696156342269786796)
XLA Ops:
  0.0 1.1 fusion.7
  1.1 0.8 fusion
  1.9 156.3 %shard_map.37 = f32[2,16,128,128]{3,2,1,0:T(8,128)} custom-call(bf16[16,512,512]{2,1,0:T(8,128)(2,1)} %bitcast.6, f32[16,512]{1,0:T(8,128)} %taps_ref.1, bf16[256,512]{1,0:T(8,128)(2,1)} %bitcast.5, bf16[16,256,1024]{2,1,0:T(8,128)(2,1)} %bitcast.7), custom_call_target="tpu_custom_call" | custom-call | flops 12999999488 | bytes 20971520 | tf_op jit(solution)/shard_map/pallas_call | solution.py:285
  158.1 3.1 %copy.5 = f32[2,16,128,128]{3,2,1,0:T(8,128)} copy(f32[2,16,128,128]{3,2,1,0:T(8,128)} %shard_map.37) | data formatting | bytes 4194304
  (1 shorter events, 0.0 us)

commit v2 on v1

v2 whole, which is shorter than its diff:
```python
import math

import jax
import jax.numpy as jnp
import numpy as np
from jax import lax
from jax.experimental import pallas as pl
from jax.experimental.pallas import tpu as pltpu
from jax.sharding import PartitionSpec as P

NFFT = 512
TAPS = 16
KB = 128
KLO = 64
APER = 1024
FRAMES = 128
SLOW = 128

BLOCK = 16
SPAN = 31
CHUNK = 128
CHUNKS = 4
TM = 8
BINS = 16
HALF = 8

MESH = pl.DeviceIdType.MESH
f32 = jnp.float32
bf16 = jnp.bfloat16

OFFSETS = ((0, 1), (1, 0), (3, 0), (2, 1), (1, 1), (2, 0), (3, 1))


def dft_table():
    sample_index = np.arange(NFFT, dtype=np.int32)
    bin_index = np.arange(KB, dtype=np.int32) + KLO
    phases = (bin_index[:, None] * sample_index[None, :] % NFFT).astype(np.float32)
    phases = phases * np.float32(2.0 * math.pi / NFFT)
    fourier = np.stack([np.cos(phases), -np.sin(phases)], 0) / np.float32(math.sqrt(NFFT))
    fourier = fourier.reshape(2, TM, 2, HALF, NFFT).transpose(1, 2, 0, 3, 4)
    return jnp.asarray(fourier.reshape(2 * KB, NFFT), bf16)


def shifted(tm, dy, flip, sign):
    y, lo = tm // 2, tm % 2
    y = lax.rem(y + (dy if sign > 0 else 4 - dy), 4)
    return 2 * y + (1 - lo if flip else lo)


def kernel(
    x_ref, taps_ref, fourier_ref, steer_ref, out_ref,
    xb, wide, filt, send, recv, steer, spec, off_out, off_in, on_out, on_in, back_out, back_in,
    x_sem, steer_sem, own_sem, send_sem, recv_sem, off_ssem, off_rsem, on_ssem, on_rsem, back_sem,
):
    tm = lax.axis_index("tm")
    fibre = lax.axis_index("fibre")
    core = fibre % 2
    hi = (fibre // 2) % 2
    count = 16
    flipped = tm + 1 - 2 * (tm % 2)
    partner = fibre + 1 - 2 * core
    outer = lax.rem(fibre + count - 1 + 2 * core, count)
    across = fibre + 2 - 4 * hi

    def there(tm_index, fibre_index):
        return {"fibre": fibre_index, "tm": tm_index}

    def chunk_of(step):
        return jnp.where(core == 0, step, CHUNKS - 1 - step)

    def x_copy(step):
        column = pl.multiple_of(chunk_of(step) * CHUNK, CHUNK)
        slot = step % 2
        return pltpu.make_async_copy(
            x_ref.at[:, :, pl.ds(column, CHUNK)], xb.at[slot], x_sem.at[slot]
        )

    quarter = HALF // 2
    steer_copy = pltpu.make_async_copy(
        steer_ref.at[pl.ds(hi * HALF, HALF)], steer.at[pl.ds(0, HALF)], steer_sem.at[0]
    )
    steer_swap = pltpu.make_async_remote_copy(
        src_ref=steer_ref.at[pl.ds(hi * HALF + core * quarter, quarter)],
        dst_ref=steer.at[pl.ds(HALF + core * quarter, quarter)],
        send_sem=steer_sem.at[1],
        recv_sem=steer_sem.at[2],
        device_id=there(flipped, across),
        device_id_type=MESH,
    )

    def steer_share(who):
        part = steer.at[pl.ds(HALF + who * quarter, quarter)]
        return pltpu.make_async_remote_copy(
            src_ref=part,
            dst_ref=part,
            send_sem=steer_sem.at[3],
            recv_sem=steer_sem.at[4],
            device_id=there(tm, partner),
            device_id_type=MESH,
        )

    x_copy(0).start()
    steer_copy.start()

    barrier = pltpu.get_barrier_semaphore()
    for dy, flip in OFFSETS:
        pl.semaphore_signal(
            barrier, inc=1, device_id=there(shifted(tm, dy, flip, 1), fibre), device_id_type=MESH
        )
    for other in (there(tm, partner), there(flipped, outer), there(flipped, across)):
        pl.semaphore_signal(barrier, inc=1, device_id=other, device_id_type=MESH)

    wide[...] = jnp.broadcast_to(taps_ref[...][:, :, None], (TAPS, NFFT, CHUNK))
    filt[:, SPAN * CHUNK :] = jnp.zeros((NFFT, CHUNK), bf16)
    recv[:, :, :, SPAN:] = jnp.zeros((CHUNKS, 2, TM, 1, 2 * HALF, CHUNK), bf16)

    frames = pl.ds(0, SPAN)

    def to_peer(step, part, index):
        dy, flip = OFFSETS[index]
        target = shifted(tm, dy, flip, 1)
        return pltpu.make_async_remote_copy(
            src_ref=send.at[step, part, target, frames],
            dst_ref=recv.at[step, part, tm, frames],
            send_sem=send_sem.at[step, part, index],
            recv_sem=recv_sem.at[step, part, index],
            device_id=there(target, fibre),
            device_id_type=MESH,
        )

    def from_peer(step, part, index):
        dy, flip = OFFSETS[index]
        source = shifted(tm, dy, flip, -1)
        return pltpu.make_async_remote_copy(
            src_ref=send.at[step, part, source, frames],
            dst_ref=recv.at[step, part, source, frames],
            send_sem=send_sem.at[step, part, index],
            recv_sem=recv_sem.at[step, part, index],
            device_id=there(source, fibre),
            device_id_type=MESH,
        )

    def own_copy(step, part):
        return pltpu.make_async_copy(
            send.at[step, part, tm, frames], recv.at[step, part, tm, frames], own_sem.at[step, part]
        )

    def send_all(step, part):
        for index in range(len(OFFSETS)):
            to_peer(step, part, index).start()
        own_copy(step, part).start()

    def off_copy(aperture, part, landing):
        return pltpu.make_async_remote_copy(
            src_ref=off_out.at[aperture, part],
            dst_ref=off_in.at[aperture, landing],
            send_sem=off_ssem.at[aperture, part],
            recv_sem=off_rsem.at[aperture, landing],
            device_id=there(flipped, outer),
            device_id_type=MESH,
        )

    def on_copy(aperture, part):
        return pltpu.make_async_remote_copy(
            src_ref=on_out.at[aperture, part],
            dst_ref=on_in.at[aperture, part],
            send_sem=on_ssem.at[aperture, part],
            recv_sem=on_rsem.at[aperture, part],
            device_id=there(tm, partner),
            device_id_type=MESH,
        )

    back_copy = pltpu.make_async_remote_copy(
        src_ref=back_out,
        dst_ref=back_in,
        send_sem=back_sem.at[0],
        recv_sem=back_sem.at[1],
        device_id=there(flipped, fibre),
        device_id_type=MESH,
    )

    parts = [jnp.where(hi == h, 0, 1) for h in range(2)]
    targets = [[jnp.where(hi == h, t, t + 1 - 2 * (t % 2)) for h in range(2)] for t in range(TM)]

    def produce(step, carry):
        slot = step % 2
        x_copy(step).wait()

        @pl.when(step < CHUNKS - 1)
        def _():
            x_copy(step + 1).start()

        def filter_rows(index, carry):
            rows = pl.ds(pl.multiple_of(index * 16, 16), 16)
            xs = [xb[slot, g, rows, :].astype(f32) for g in range(BLOCK)]
            ts = [wide[t, rows, :] for t in range(TAPS)]
            for frame in range(SPAN):
                first, last = max(0, frame - BLOCK + 1), min(TAPS - 1, frame)
                total = ts[first] * xs[frame - first]
                for t in range(first + 1, last + 1):
                    total = total + ts[t] * xs[frame - t]
                filt[rows, frame * CHUNK : (frame + 1) * CHUNK] = total.astype(bf16)
            return carry

        lax.fori_loop(0, NFFT // 16, filter_rows, 0)

        def transform(pair, carry):
            columns = pl.ds(pl.multiple_of(pair * 2 * CHUNK, 2 * CHUNK), 2 * CHUNK)
            values = jnp.dot(
                fourier_ref[...], filt[:, columns], preferred_element_type=f32
            ).astype(bf16)
            for side_frame in range(2):
                for t in range(TM):
                    for h in range(2):
                        row = (2 * t + h) * 2 * HALF
                        send[step, parts[h], targets[t][h], pair * 2 + side_frame] = values[
                            row : row + 2 * HALF, side_frame * CHUNK : (side_frame + 1) * CHUNK
                        ]
            return carry

        lax.fori_loop(0, (SPAN + 1) // 2, transform, 0)

        @pl.when(step == 0)
        def _():
            pl.semaphore_wait(barrier, len(OFFSETS) + 3)
            steer_swap.start()

        send_all(step, 1)

        @pl.when(step < 2)
        def _():
            send_all(step, 0)

        return carry

    lax.fori_loop(0, CHUNKS, produce, 0)
    send_all(2, 0)
    send_all(3, 0)

    def combine(step, part):
        for index in range(len(OFFSETS)):
            from_peer(step, part, index).wait_recv()
        own_copy(step, part).wait()
        columns = pl.ds(pl.multiple_of(chunk_of(step) * CHUNK, CHUNK), CHUNK)

        def block(i, carry):
            before = jnp.maximum(i - 1, 0)
            late = recv[step, part, before, pl.ds(BLOCK, BLOCK)].astype(f32)
            total = recv[step, part, i, pl.ds(0, BLOCK)].astype(f32) + jnp.where(i > 0, late, 0.0)
            turned = jnp.transpose(total, (1, 0, 2)).astype(bf16)
            for p in range(2):
                rows = pl.ds(pl.multiple_of(p * FRAMES + i * BLOCK, BLOCK), BLOCK)
                spec[pl.ds(part * HALF, HALF), rows, columns] = turned[p * HALF : (p + 1) * HALF]
            return carry

        lax.fori_loop(0, TM, block, 0)

    def product(k, u, width, m):
        if not isinstance(u, int):
            u, m = pl.multiple_of(u, CHUNK), pl.multiple_of(m, CHUNK)
        left = spec[k, :, pl.ds(u, width)]
        right = steer[k, :, pl.ds(m, width)]
        values = lax.dot_general(
            left, right, (((1,), (1,)), ((), ())), preferred_element_type=f32
        )
        real = values[:FRAMES, :SLOW] - values[FRAMES:, SLOW:]
        imag = values[FRAMES:, :SLOW] + values[:FRAMES, SLOW:]
        return real, imag

    def side(out, aperture, part, to_left, width):
        u = jnp.where(to_left, 0, 512 - width)
        m = jnp.where(to_left, APER - width, 0)

        def one(k, carry):
            real, imag = product(part * HALF + k, u, width, m)
            out[aperture, part, k, 0] = real.astype(bf16)
            out[aperture, part, k, 1] = imag.astype(bf16)
            return carry

        lax.fori_loop(0, HALF, one, 0)

    def off_near(part):
        side(off_out, core, part, core == 0, 128)
        off_copy(core, part, 1 - part).start()

    def off_far(part):
        side(off_out, 1 - core, part, core == 0, 384)
        off_copy(1 - core, part, 1 - part).start()

    def on_chip(part):
        side(on_out, 1 - core, part, core == 1, 128)
        on_copy(1 - core, part).start()
        side(on_out, core, part, core == 1, 384)
        on_copy(core, part).start()

    def own(part):
        def one(k, carry):
            k = part * HALF + k
            for aperture in range(2):
                real, imag = product(k, 0, 512, 384 - 256 * aperture)
                wide[k, pl.ds(aperture * 256, 128)] = real
                wide[k, pl.ds(aperture * 256 + 128, 128)] = imag
            return carry

        lax.fori_loop(0, HALF, one, 0)

    inside = jnp.logical_and(
        jnp.logical_or(fibre > 0, core == 1), jnp.logical_or(fibre < count - 1, core == 0)
    )

    def power(part, aperture, k):
        squares = []
        for piece in range(2):
            total = wide[part * HALF + k, pl.ds(aperture * 256 + piece * 128, 128)]
            total = total + on_in[aperture, part, k, piece].astype(f32)
            far = off_in[aperture, part, k, piece].astype(f32)
            total = total + jnp.where(inside, far, 0.0)
            squares.append(total * total)
        return squares[0] + squares[1]

    def wait_sides(part):
        for aperture in range(2):
            on_copy(aperture, part).wait_recv()
            off_copy(aperture, 1 - part, part).wait_recv()

    combine(0, 1)
    combine(0, 0)
    steer_copy.wait()
    off_near(0)
    steer_swap.wait()
    steer_share(core).start()
    combine(1, 1)
    combine(1, 0)
    steer_share(1 - core).wait_recv()
    off_near(1)
    combine(2, 1)
    off_far(1)
    combine(3, 1)
    on_chip(1)
    own(1)
    combine(2, 0)
    off_far(0)
    wait_sides(1)

    def finish_other(k, carry):
        for aperture in range(2):
            back_out[aperture, k] = power(1, aperture, k).astype(bf16)
        return carry

    lax.fori_loop(0, HALF, finish_other, 0)
    back_copy.start()

    combine(3, 0)
    on_chip(0)
    own(0)
    wait_sides(0)

    def finish_own(k, carry):
        for aperture in range(2):
            out_ref[aperture, hi * HALF + k] = power(0, aperture, k)
        return carry

    lax.fori_loop(0, HALF, finish_own, 0)

    back_copy.wait()

    def place(k, carry):
        for aperture in range(2):
            out_ref[aperture, (1 - hi) * HALF + k] = back_in[aperture, k].astype(f32)
        return carry

    lax.fori_loop(0, HALF, place, 0)

    steer_share(core).wait_send()
    for part in range(2):
        for aperture in range(2):
            on_copy(aperture, part).wait_send()
            off_copy(aperture, part, 1 - part).wait_send()

    def drain(step, carry):
        for part in range(2):
            for index in range(len(OFFSETS)):
                to_peer(step, part, index).wait_send()
        return carry

    lax.fori_loop(0, CHUNKS, drain, 0)


def body(samples, filter_taps, steering):
    peers = len(OFFSETS)
    vmem = pl.BlockSpec(memory_space=pltpu.VMEM)
    hbm = pl.BlockSpec(memory_space=pl.ANY)
    dma = pltpu.SemaphoreType.DMA
    return pl.pallas_call(
        kernel,
        out_shape=jax.ShapeDtypeStruct((2, BINS, FRAMES, SLOW), f32),
        in_specs=[hbm, vmem, vmem, hbm],
        out_specs=vmem,
        scratch_shapes=[
            pltpu.VMEM((2, BLOCK, NFFT, CHUNK), bf16),
            pltpu.VMEM((TAPS, NFFT, CHUNK), f32),
            pltpu.VMEM((NFFT, (SPAN + 1) * CHUNK), bf16),
            pltpu.VMEM((CHUNKS, 2, TM, SPAN + 1, 2 * HALF, CHUNK), bf16),
            pltpu.VMEM((CHUNKS, 2, TM, SPAN + 1, 2 * HALF, CHUNK), bf16),
            pltpu.VMEM((BINS, 2 * SLOW, APER), bf16),
            pltpu.VMEM((BINS, 2 * FRAMES, CHUNKS * CHUNK), bf16),
            pltpu.VMEM((2, 2, HALF, 2, FRAMES, SLOW), bf16),
            pltpu.VMEM((2, 2, HALF, 2, FRAMES, SLOW), bf16),
            pltpu.VMEM((2, 2, HALF, 2, FRAMES, SLOW), bf16),
            pltpu.VMEM((2, 2, HALF, 2, FRAMES, SLOW), bf16),
            pltpu.VMEM((2, HALF, FRAMES, SLOW), bf16),
            pltpu.VMEM((2, HALF, FRAMES, SLOW), bf16),
            dma((2,)),
            dma((5,)),
            dma((CHUNKS, 2)),
            dma((CHUNKS, 2, peers)),
            dma((CHUNKS, 2, peers)),
            dma((2, 2)),
            dma((2, 2)),
            dma((2, 2)),
            dma((2, 2)),
            dma((2,)),
        ],
        compiler_params=pltpu.CompilerParams(
            collective_id=0, has_side_effects=True, vmem_limit_bytes=60 * 2**20
        ),
        cost_estimate=pl.CostEstimate(
            flops=13 * 10**9, bytes_accessed=20 * 2**20, transcendentals=0
        ),
    )(
        samples.reshape(BLOCK, NFFT, samples.shape[1]),
        filter_taps,
        dft_table(),
        steering.reshape(BINS, 2 * SLOW, APER),
    )


def solution(mesh):
    in_specs = (P("tm", "fibre"), P(), P("tm", None, None, None))
    out_specs = P("fibre", "tm", None, None)
    return jax.shard_map(body, mesh=mesh, in_specs=in_specs, out_specs=out_specs, check_vma=False)
```

time: 161 us -> 129 us (0.80)
  Pallas kernels: 156 us -> 125 us
  other arithmetic: 1.86 us -> 0 us
    pallas_call x1, Pallas kernels: 156 us -> 125 us  [body(): pl.pallas_call(kernel, out_shape=jax.ShapeDtypeStruct((2, BINS, FRAMES, S...]
where the time goes in v2:
time: 129 us
  Pallas kernels  125 us (97%)
  local copies, waits for them, and re-layouts  3.14 us (2%)
    pallas_call x1, Pallas kernels, body(): pl.pallas_call(kernel, out_shape=jax.ShapeDtypeStruct((2, BINS, FRAMES, S...  125 us
    unnamed x1, local copies, waits for them, and re-layouts  3.14 us

profile of v2, /device:TPU:1, one launch (start us, length us, event | category | flops | bytes accessed | tf_op | source)
XLA Modules:
  0.0 128.6 jit_solution(8415216797759107425)
XLA Ops:
  0.0 125.4 %shard_map.46 = f32[2,16,128,128]{3,2,1,0:T(8,128)} custom-call(bf16[16,512,512]{2,1,0:T(8,128)(2,1)} %bitcast.2, f32[16,512]{1,0:T(8,128)} %taps_ref.1, bf16[256,512]{1,0:T(8,128)(2,1)} %constant.2.clone.fourier_ref, bf16[16,256,1024]{2,1,0:T(8,128)(2,1)} %bitcast.3), custom_call_target="tpu_custom_call" | custom-call | flops 12999999488 | bytes 20971520 | tf_op jit(solution)/shard_map/pallas_call | solution.py:394
  125.4 3.1 %copy.6 = f32[2,16,128,128]{3,2,1,0:T(8,128)} copy(f32[2,16,128,128]{3,2,1,0:T(8,128)} %shard_map.46) | data formatting | bytes 4194304

commit v3 on v2

--- a/solution.py
+++ b/solution.py
@@ -23,6 +23,7 @@
 TM = 8
 BINS = 16
 HALF = 8
+GROUPS = ((0, 8), (8, 16), (16, 24), (24, 31))
 
 MESH = pl.DeviceIdType.MESH
 f32 = jnp.float32
@@ -41,10 +42,12 @@
     return jnp.asarray(fourier.reshape(2 * KB, NFFT), bf16)
 
 
-def shifted(tm, dy, flip, sign):
-    y, lo = tm // 2, tm % 2
-    y = lax.rem(y + (dy if sign > 0 else 4 - dy), 4)
-    return 2 * y + (1 - lo if flip else lo)
+def peer(tm, core, index, sign):
+    (dy0, flip0), (dy1, flip1) = OFFSETS[index], OFFSETS[len(OFFSETS) - 1 - index]
+    dy, flip = jnp.where(core == 0, dy0, dy1), jnp.where(core == 0, flip0, flip1)
+    lo = tm % 2
+    y = lax.rem(tm // 2 + (dy if sign > 0 else 4 - dy), 4)
+    return 2 * y + lo + flip - 2 * lo * flip
 
 
 def kernel(
@@ -75,6 +78,13 @@
             x_ref.at[:, :, pl.ds(column, CHUNK)], xb.at[slot], x_sem.at[slot]
         )
 
+    def x_first(number):
+        column = pl.multiple_of(chunk_of(0) * CHUNK, CHUNK)
+        some = pl.ds(number * (BLOCK // 2), BLOCK // 2)
+        return pltpu.make_async_copy(
+            x_ref.at[some, :, pl.ds(column, CHUNK)], xb.at[0, some], x_sem.at[2 * number]
+        )
+
     quarter = HALF // 2
     steer_copy = pltpu.make_async_copy(
         steer_ref.at[pl.ds(hi * HALF, HALF)], steer.at[pl.ds(0, HALF)], steer_sem.at[0]
@@ -99,50 +109,57 @@
             device_id_type=MESH,
         )
 
-    x_copy(0).start()
+    x_first(0).start()
+    x_first(1).start()
     steer_copy.start()
 
     barrier = pltpu.get_barrier_semaphore()
-    for dy, flip in OFFSETS:
+    for index in range(len(OFFSETS)):
         pl.semaphore_signal(
-            barrier, inc=1, device_id=there(shifted(tm, dy, flip, 1), fibre), device_id_type=MESH
+            barrier, inc=1, device_id=there(peer(tm, core, index, 1), fibre), device_id_type=MESH
         )
     for other in (there(tm, partner), there(flipped, outer), there(flipped, across)):
         pl.semaphore_signal(barrier, inc=1, device_id=other, device_id_type=MESH)
 
     wide[...] = jnp.broadcast_to(taps_ref[...][:, :, None], (TAPS, NFFT, CHUNK))
     filt[:, SPAN * CHUNK :] = jnp.zeros((NFFT, CHUNK), bf16)
-    recv[:, :, :, SPAN:] = jnp.zeros((CHUNKS, 2, TM, 1, 2 * HALF, CHUNK), bf16)
-
-    frames = pl.ds(0, SPAN)
-
-    def to_peer(step, part, index):
-        dy, flip = OFFSETS[index]
-        target = shifted(tm, dy, flip, 1)
+    recv[:, :, :, SPAN:] = jnp.zeros((CHUNKS, TM, 2, 1, 2 * HALF, CHUNK), bf16)
+
+    whole = (0, SPAN)
+
+    def piece(ref, step, device, part, frames):
+        sets = pl.ds(0, 2) if part is None else pl.ds(part, 1)
+        return ref.at[step, device, sets, pl.ds(frames[0], frames[1] - frames[0])]
+
+    def to_peer(step, part, index, frames=whole):
+        target = peer(tm, core, index, 1)
+        slot = 0 if part is None else part
         return pltpu.make_async_remote_copy(
-            src_ref=send.at[step, part, target, frames],
-            dst_ref=recv.at[step, part, tm, frames],
-            send_sem=send_sem.at[step, part, index],
-            recv_sem=recv_sem.at[step, part, index],
+            src_ref=piece(send, step, target, part, frames),
+            dst_ref=piece(recv, step, tm, part, frames),
+            send_sem=send_sem.at[step, slot, index],
+            recv_sem=recv_sem.at[step, slot, index],
             device_id=there(target, fibre),
             device_id_type=MESH,
         )
 
     def from_peer(step, part, index):
-        dy, flip = OFFSETS[index]
-        source = shifted(tm, dy, flip, -1)
+        source = peer(tm, core, index, -1)
+        slot = 0 if part is None else part
         return pltpu.make_async_remote_copy(
-            src_ref=send.at[step, part, source, frames],
-            dst_ref=recv.at[step, part, source, frames],
-            send_sem=send_sem.at[step, part, index],
-            recv_sem=recv_sem.at[step, part, index],
+            src_ref=piece(send, step, source, part, whole),
+            dst_ref=piece(recv, step, source, part, whole),
+            send_sem=send_sem.at[step, slot, index],
+            recv_sem=recv_sem.at[step, slot, index],
             device_id=there(source, fibre),
             device_id_type=MESH,
         )
 
     def own_copy(step, part):
         return pltpu.make_async_copy(
-            send.at[step, part, tm, frames], recv.at[step, part, tm, frames], own_sem.at[step, part]
+            piece(send, step, tm, part, whole),
+            piece(recv, step, tm, part, whole),
+            own_sem.at[step, 0 if part is None else part],
         )
 
     def send_all(step, part):
@@ -182,19 +199,14 @@
     parts = [jnp.where(hi == h, 0, 1) for h in range(2)]
     targets = [[jnp.where(hi == h, t, t + 1 - 2 * (t % 2)) for h in range(2)] for t in range(TM)]
 
-    def produce(step, carry):
-        slot = step % 2
-        x_copy(step).wait()
-
-        @pl.when(step < CHUNKS - 1)
-        def _():
-            x_copy(step + 1).start()
+    def filter_frames(slot, frames):
+        first_x, last_x = max(0, frames[0] - TAPS + 1), min(BLOCK, frames[1])
 
         def filter_rows(index, carry):
             rows = pl.ds(pl.multiple_of(index * 16, 16), 16)
-            xs = [xb[slot, g, rows, :].astype(f32) for g in range(BLOCK)]
+            xs = {g: xb[slot, g, rows, :].astype(f32) for g in range(first_x, last_x)}
             ts = [wide[t, rows, :] for t in range(TAPS)]
-            for frame in range(SPAN):
+            for frame in range(*frames):
                 first, last = max(0, frame - BLOCK + 1), min(TAPS - 1, frame)
                 total = ts[first] * xs[frame - first]
                 for t in range(first + 1, last + 1):
@@ -204,49 +216,74 @@
 
         lax.fori_loop(0, NFFT // 16, filter_rows, 0)
 
+    def transform_frames(step, frames):
         def transform(pair, carry):
             columns = pl.ds(pl.multiple_of(pair * 2 * CHUNK, 2 * CHUNK), 2 * CHUNK)
             values = jnp.dot(
                 fourier_ref[...], filt[:, columns], preferred_element_type=f32
             ).astype(bf16)
-            for side_frame in range(2):
+            for odd in range(2):
                 for t in range(TM):
                     for h in range(2):
                         row = (2 * t + h) * 2 * HALF
-                        send[step, parts[h], targets[t][h], pair * 2 + side_frame] = values[
-                            row : row + 2 * HALF, side_frame * CHUNK : (side_frame + 1) * CHUNK
+                        send[step, targets[t][h], parts[h], pair * 2 + odd] = values[
+                            row : row + 2 * HALF, odd * CHUNK : (odd + 1) * CHUNK
                         ]
             return carry
 
-        lax.fori_loop(0, (SPAN + 1) // 2, transform, 0)
-
-        @pl.when(step == 0)
+        lax.fori_loop(frames[0] // 2, (frames[1] + 1) // 2, transform, 0)
+
+    for number, frames in enumerate(GROUPS):
+        if number < 2:
+            x_first(number).wait()
+        if number == 1:
+            x_copy(1).start()
+        filter_frames(0, frames)
+        transform_frames(0, frames)
+        if number == 0:
+            pl.semaphore_wait(barrier, len(OFFSETS) + 3)
+        for index in range(len(OFFSETS)):
+            to_peer(0, None, index, frames).start()
+        if number == 0:
+            steer_swap.start()
+    own_copy(0, None).start()
+
+    def produce(step, carry):
+        x_copy(step).wait()
+
+        @pl.when(step < CHUNKS - 1)
         def _():
-            pl.semaphore_wait(barrier, len(OFFSETS) + 3)
-            steer_swap.start()
-
-        send_all(step, 1)
-
-        @pl.when(step < 2)
+            x_copy(step + 1).start()
+
+        filter_frames(step % 2, whole)
+        transform_frames(step, whole)
+
+        @pl.when(step == 1)
         def _():
-            send_all(step, 0)
+            send_all(1, None)
+
+        @pl.when(step > 1)
+        def _():
+            send_all(step, 1)
 
         return carry
 
-    lax.fori_loop(0, CHUNKS, produce, 0)
+    lax.fori_loop(1, CHUNKS, produce, 0)
     send_all(2, 0)
     send_all(3, 0)
 
-    def combine(step, part):
+    def arrive(step, part):
         for index in range(len(OFFSETS)):
             from_peer(step, part, index).wait_recv()
         own_copy(step, part).wait()
+
+    def combine(step, part):
         columns = pl.ds(pl.multiple_of(chunk_of(step) * CHUNK, CHUNK), CHUNK)
 
         def block(i, carry):
             before = jnp.maximum(i - 1, 0)
-            late = recv[step, part, before, pl.ds(BLOCK, BLOCK)].astype(f32)
-            total = recv[step, part, i, pl.ds(0, BLOCK)].astype(f32) + jnp.where(i > 0, late, 0.0)
+            late = recv[step, before, part, pl.ds(BLOCK, BLOCK)].astype(f32)
+            total = recv[step, i, part, pl.ds(0, BLOCK)].astype(f32) + jnp.where(i > 0, late, 0.0)
             turned = jnp.transpose(total, (1, 0, 2)).astype(bf16)
             for p in range(2):
                 rows = pl.ds(pl.multiple_of(p * FRAMES + i * BLOCK, BLOCK), BLOCK)
@@ -323,21 +360,26 @@
             on_copy(aperture, part).wait_recv()
             off_copy(aperture, 1 - part, part).wait_recv()
 
-    combine(0, 1)
+    arrive(0, None)
     combine(0, 0)
     steer_copy.wait()
     off_near(0)
+    combine(0, 1)
     steer_swap.wait()
     steer_share(core).start()
+    arrive(1, None)
     combine(1, 1)
     combine(1, 0)
     steer_share(1 - core).wait_recv()
     off_near(1)
+    arrive(2, 1)
     combine(2, 1)
     off_far(1)
+    arrive(3, 1)
     combine(3, 1)
     on_chip(1)
     own(1)
+    arrive(2, 0)
     combine(2, 0)
     off_far(0)
     wait_sides(1)
@@ -350,6 +392,7 @@
     lax.fori_loop(0, HALF, finish_other, 0)
     back_copy.start()
 
+    arrive(3, 0)
     combine(3, 0)
     on_chip(0)
     own(0)
@@ -377,13 +420,17 @@
             on_copy(aperture, part).wait_send()
             off_copy(aperture, part, 1 - part).wait_send()
 
-    def drain(step, carry):
-        for part in range(2):
-            for index in range(len(OFFSETS)):
-                to_peer(step, part, index).wait_send()
-        return carry
-
-    lax.fori_loop(0, CHUNKS, drain, 0)
+    def drain(index_of_parts, steps):
+        def one(step, carry):
+            for part in index_of_parts:
+                for index in range(len(OFFSETS)):
+                    to_peer(step, part, index).wait_send()
+            return carry
+
+        lax.fori_loop(*steps, one, 0)
+
+    drain((None,), (0, 2))
+    drain((0, 1), (2, CHUNKS))
 
 
 def body(samples, filter_taps, steering):
@@ -400,8 +447,8 @@
             pltpu.VMEM((2, BLOCK, NFFT, CHUNK), bf16),
             pltpu.VMEM((TAPS, NFFT, CHUNK), f32),
             pltpu.VMEM((NFFT, (SPAN + 1) * CHUNK), bf16),
-            pltpu.VMEM((CHUNKS, 2, TM, SPAN + 1, 2 * HALF, CHUNK), bf16),
-            pltpu.VMEM((CHUNKS, 2, TM, SPAN + 1, 2 * HALF, CHUNK), bf16),
+            pltpu.VMEM((CHUNKS, TM, 2, SPAN + 1, 2 * HALF, CHUNK), bf16),
+            pltpu.VMEM((CHUNKS, TM, 2, SPAN + 1, 2 * HALF, CHUNK), bf16),
             pltpu.VMEM((BINS, 2 * SLOW, APER), bf16),
             pltpu.VMEM((BINS, 2 * FRAMES, CHUNKS * CHUNK), bf16),
             pltpu.VMEM((2, 2, HALF, 2, FRAMES, SLOW), bf16),
@@ -410,7 +457,7 @@
             pltpu.VMEM((2, 2, HALF, 2, FRAMES, SLOW), bf16),
             pltpu.VMEM((2, HALF, FRAMES, SLOW), bf16),
             pltpu.VMEM((2, HALF, FRAMES, SLOW), bf16),
-            dma((2,)),
+            dma((3,)),
             dma((5,)),
             dma((CHUNKS, 2)),
             dma((CHUNKS, 2, peers)),

time: 129 us -> 119 us (0.922)
  Pallas kernels: 125 us -> 116 us
    pallas_call x1, Pallas kernels: 125 us -> 116 us  [body(): pl.pallas_call(kernel, out_shape=jax.ShapeDtypeStruct((2, BINS, FRAMES, S...]
where the time goes in v3:
time: 119 us
  Pallas kernels  116 us (97%)
  local copies, waits for them, and re-layouts  3.14 us (3%)
    pallas_call x1, Pallas kernels, body(): pl.pallas_call(kernel, out_shape=jax.ShapeDtypeStruct((2, BINS, FRAMES, S...  116 us
    unnamed x1, local copies, waits for them, and re-layouts  3.14 us

profile of v3, /device:TPU:1, one launch (start us, length us, event | category | flops | bytes accessed | tf_op | source)
XLA Modules:
  0.0 119.2 jit_solution(11003431342065400827)
XLA Ops:
  0.0 116.0 %shard_map.46 = f32[2,16,128,128]{3,2,1,0:T(8,128)} custom-call(bf16[16,512,512]{2,1,0:T(8,128)(2,1)} %bitcast.2, f32[16,512]{1,0:T(8,128)} %taps_ref.1, bf16[256,512]{1,0:T(8,128)(2,1)} %constant.2.clone.fourier_ref, bf16[16,256,1024]{2,1,0:T(8,128)(2,1)} %bitcast.3), custom_call_target="tpu_custom_call" | custom-call | flops 12999999488 | bytes 20971520 | tf_op jit(solution)/shard_map/pallas_call | solution.py:441
  116.0 3.1 %copy.6 = f32[2,16,128,128]{3,2,1,0:T(8,128)} copy(f32[2,16,128,128]{3,2,1,0:T(8,128)} %shard_map.46) | data formatting | bytes 4194304

commit v4 on v3

--- a/solution.py
+++ b/solution.py
@@ -23,13 +23,14 @@
 TM = 8
 BINS = 16
 HALF = 8
-GROUPS = ((0, 8), (8, 16), (16, 24), (24, 31))
+GROUPS = ((0, 4), (4, 8), (8, 16), (16, 24), (24, 31))
 
 MESH = pl.DeviceIdType.MESH
 f32 = jnp.float32
 bf16 = jnp.bfloat16
 
-OFFSETS = ((0, 1), (1, 0), (3, 0), (2, 1), (1, 1), (2, 0), (3, 1))
+OFFSETS = ((2, 1), (0, 1), (2, 0), (1, 1), (1, 0), (3, 1), (3, 0))
+OFFSETS1 = ((3, 0), (3, 1), (1, 0), (1, 1), (2, 0), (0, 1), (2, 1))
 
 
 def dft_table():
@@ -43,7 +44,7 @@
 
 
 def peer(tm, core, index, sign):
-    (dy0, flip0), (dy1, flip1) = OFFSETS[index], OFFSETS[len(OFFSETS) - 1 - index]
+    (dy0, flip0), (dy1, flip1) = OFFSETS[index], OFFSETS1[index]
     dy, flip = jnp.where(core == 0, dy0, dy1), jnp.where(core == 0, flip0, flip1)
     lo = tm % 2
     y = lax.rem(tm // 2 + (dy if sign > 0 else 4 - dy), 4)
@@ -234,9 +235,9 @@
         lax.fori_loop(frames[0] // 2, (frames[1] + 1) // 2, transform, 0)
 
     for number, frames in enumerate(GROUPS):
-        if number < 2:
-            x_first(number).wait()
-        if number == 1:
+        if number == 0 or number == 2:
+            x_first(number // 2).wait()
+        if number == 2:
             x_copy(1).start()
         filter_frames(0, frames)
         transform_frames(0, frames)
@@ -266,10 +267,13 @@
         def _():
             send_all(step, 1)
 
+        @pl.when(step == 2)
+        def _():
+            send_all(2, 0)
+
         return carry
 
     lax.fori_loop(1, CHUNKS, produce, 0)
-    send_all(2, 0)
     send_all(3, 0)
 
     def arrive(step, part):
@@ -375,13 +379,13 @@
     arrive(2, 1)
     combine(2, 1)
     off_far(1)
+    arrive(2, 0)
+    combine(2, 0)
+    off_far(0)
     arrive(3, 1)
     combine(3, 1)
     on_chip(1)
     own(1)
-    arrive(2, 0)
-    combine(2, 0)
-    off_far(0)
     wait_sides(1)
 
     def finish_other(k, carry):
@@ -440,7 +444,7 @@
     dma = pltpu.SemaphoreType.DMA
     return pl.pallas_call(
         kernel,
-        out_shape=jax.ShapeDtypeStruct((2, BINS, FRAMES, SLOW), f32),
+        out_shape=pltpu.VMEM((2, BINS, FRAMES, SLOW), f32),
         in_specs=[hbm, vmem, vmem, hbm],
         out_specs=vmem,
         scratch_shapes=[

time: 119 us -> 111 us (0.933)
  Pallas kernels: 116 us -> 110 us
  local copies, waits for them, and re-layouts: 3.14 us -> 1.32 us
    pallas_call x1, Pallas kernels: 116 us -> 110 us  [body(): pl.pallas_call(kernel, out_shape=pltpu.VMEM((2, BINS, FRAMES, SLOW), f32)...]
    unnamed x1, local copies, waits for them, and re-layouts: 3.14 us -> 1.32 us
where the time goes in v4:
time: 111 us
  Pallas kernels  110 us (99%)
  local copies, waits for them, and re-layouts  1.32 us (1%)
    pallas_call x1, Pallas kernels, body(): pl.pallas_call(kernel, out_shape=pltpu.VMEM((2, BINS, FRAMES, SLOW), f32)...  110 us

profile of v4, /device:TPU:1, one launch (start us, length us, event | category | flops | bytes accessed | tf_op | source)
XLA Modules:
  0.0 111.2 jit_solution(12405698002316312026)
XLA Ops:
  0.0 109.9 %shard_map.46 = f32[2,16,128,128]{3,2,1,0:T(8,128)S(1)} custom-call(bf16[16,512,512]{2,1,0:T(8,128)(2,1)} %bitcast.2, f32[16,512]{1,0:T(8,128)} %taps_ref.1, bf16[256,512]{1,0:T(8,128)(2,1)} %constant.2.clone.fourier_ref, bf16[16,256,1024]{2,1,0:T(8,128)(2,1)} %bitcast.3), custom_call_target="tpu_custom_call" | custom-call | flops 12999999488 | bytes 20971520 | tf_op jit(solution)/shard_map/pallas_call | solution.py:445
  109.9 1.3 %copy.6 = f32[2,16,128,128]{3,2,1,0:T(8,128)} copy(f32[2,16,128,128]{3,2,1,0:T(8,128)S(1)} %shard_map.46) | data formatting | bytes 4194304

commit v5 on v4

--- a/solution.py
+++ b/solution.py
@@ -60,11 +60,17 @@
     fibre = lax.axis_index("fibre")
     core = fibre % 2
     hi = (fibre // 2) % 2
+    odd_x = (fibre // 4) % 2
     count = 16
     flipped = tm + 1 - 2 * (tm % 2)
     partner = fibre + 1 - 2 * core
     outer = lax.rem(fibre + count - 1 + 2 * core, count)
     across = fibre + 2 - 4 * hi
+    beside = fibre + 4 - 8 * odd_x
+
+    inside = jnp.logical_and(
+        jnp.logical_or(fibre > 0, core == 1), jnp.logical_or(fibre < count - 1, core == 0)
+    )
 
     def there(tm_index, fibre_index):
         return {"fibre": fibre_index, "tm": tm_index}
@@ -86,29 +92,41 @@
             x_ref.at[some, :, pl.ds(column, CHUNK)], xb.at[0, some], x_sem.at[2 * number]
         )
 
-    quarter = HALF // 2
+    quarter = HALF // 4
     steer_copy = pltpu.make_async_copy(
         steer_ref.at[pl.ds(hi * HALF, HALF)], steer.at[pl.ds(0, HALF)], steer_sem.at[0]
     )
+    def quarter_of(parity, who):
+        return parity * 2 * quarter + who * quarter
+
     steer_swap = pltpu.make_async_remote_copy(
-        src_ref=steer_ref.at[pl.ds(hi * HALF + core * quarter, quarter)],
-        dst_ref=steer.at[pl.ds(HALF + core * quarter, quarter)],
+        src_ref=steer_ref.at[pl.ds(hi * HALF + quarter_of(odd_x, core), quarter)],
+        dst_ref=steer.at[pl.ds(HALF + quarter_of(odd_x, core), quarter)],
         send_sem=steer_sem.at[1],
         recv_sem=steer_sem.at[2],
         device_id=there(flipped, across),
         device_id_type=MESH,
     )
 
-    def steer_share(who):
-        part = steer.at[pl.ds(HALF + who * quarter, quarter)]
+    def steer_pass(parity, who, sem, device):
+        part = steer.at[pl.ds(HALF + quarter_of(parity, who), quarter)]
         return pltpu.make_async_remote_copy(
             src_ref=part,
             dst_ref=part,
-            send_sem=steer_sem.at[3],
-            recv_sem=steer_sem.at[4],
-            device_id=there(tm, partner),
+            send_sem=steer_sem.at[sem],
+            recv_sem=steer_sem.at[sem + 1],
+            device_id=device,
             device_id_type=MESH,
         )
+
+    def steer_beside(parity):
+        return steer_pass(parity, core, 3, there(tm, beside))
+
+    def steer_first(who):
+        return steer_pass(odd_x, who, 5, there(tm, partner))
+
+    def steer_second(who):
+        return steer_pass(1 - odd_x, who, 7, there(tm, partner))
 
     x_first(0).start()
     x_first(1).start()
@@ -119,11 +137,16 @@
         pl.semaphore_signal(
             barrier, inc=1, device_id=there(peer(tm, core, index, 1), fibre), device_id_type=MESH
         )
-    for other in (there(tm, partner), there(flipped, outer), there(flipped, across)):
+    others = (there(tm, partner), there(flipped, outer), there(flipped, across), there(tm, beside))
+    for other in others:
         pl.semaphore_signal(barrier, inc=1, device_id=other, device_id_type=MESH)
 
     wide[...] = jnp.broadcast_to(taps_ref[...][:, :, None], (TAPS, NFFT, CHUNK))
     filt[:, SPAN * CHUNK :] = jnp.zeros((NFFT, CHUNK), bf16)
+    @pl.when(jnp.logical_not(inside))
+    def _():
+        off_in[...] = jnp.zeros_like(off_in)
+
     recv[:, :, :, SPAN:] = jnp.zeros((CHUNKS, TM, 2, 1, 2 * HALF, CHUNK), bf16)
 
     whole = (0, SPAN)
@@ -242,7 +265,7 @@
         filter_frames(0, frames)
         transform_frames(0, frames)
         if number == 0:
-            pl.semaphore_wait(barrier, len(OFFSETS) + 3)
+            pl.semaphore_wait(barrier, len(OFFSETS) + len(others))
         for index in range(len(OFFSETS)):
             to_peer(0, None, index, frames).start()
         if number == 0:
@@ -251,6 +274,12 @@
 
     def produce(step, carry):
         x_copy(step).wait()
+
+        @pl.when(step == 2)
+        def _():
+            steer_swap.wait_recv()
+            steer_beside(odd_x).start()
+            steer_first(core).start()
 
         @pl.when(step < CHUNKS - 1)
         def _():
@@ -321,12 +350,16 @@
         lax.fori_loop(0, HALF, one, 0)
 
     def off_near(part):
-        side(off_out, core, part, core == 0, 128)
-        off_copy(core, part, 1 - part).start()
+        @pl.when(inside)
+        def _():
+            side(off_out, core, part, core == 0, 128)
+            off_copy(core, part, 1 - part).start()
 
     def off_far(part):
-        side(off_out, 1 - core, part, core == 0, 384)
-        off_copy(1 - core, part, 1 - part).start()
+        @pl.when(inside)
+        def _():
+            side(off_out, 1 - core, part, core == 0, 384)
+            off_copy(1 - core, part, 1 - part).start()
 
     def on_chip(part):
         side(on_out, 1 - core, part, core == 1, 128)
@@ -344,10 +377,6 @@
             return carry
 
         lax.fori_loop(0, HALF, one, 0)
-
-    inside = jnp.logical_and(
-        jnp.logical_or(fibre > 0, core == 1), jnp.logical_or(fibre < count - 1, core == 0)
-    )
 
     def power(part, aperture, k):
         squares = []
@@ -362,19 +391,24 @@
     def wait_sides(part):
         for aperture in range(2):
             on_copy(aperture, part).wait_recv()
-            off_copy(aperture, 1 - part, part).wait_recv()
+
+        @pl.when(inside)
+        def _():
+            for aperture in range(2):
+                off_copy(aperture, 1 - part, part).wait_recv()
 
     arrive(0, None)
     combine(0, 0)
     steer_copy.wait()
     off_near(0)
     combine(0, 1)
-    steer_swap.wait()
-    steer_share(core).start()
+    steer_beside(1 - odd_x).wait_recv()
+    steer_second(core).start()
     arrive(1, None)
     combine(1, 1)
     combine(1, 0)
-    steer_share(1 - core).wait_recv()
+    steer_first(1 - core).wait_recv()
+    steer_second(1 - core).wait_recv()
     off_near(1)
     arrive(2, 1)
     combine(2, 1)
@@ -418,11 +452,21 @@
 
     lax.fori_loop(0, HALF, place, 0)
 
-    steer_share(core).wait_send()
-    for part in range(2):
+    steer_swap.wait_send()
+    steer_beside(odd_x).wait_send()
+    steer_first(core).wait_send()
+    steer_second(core).wait_send()
+    def drain_sides(part):
         for aperture in range(2):
             on_copy(aperture, part).wait_send()
-            off_copy(aperture, part, 1 - part).wait_send()
+
+        @pl.when(inside)
+        def _():
+            for aperture in range(2):
+                off_copy(aperture, part, 1 - part).wait_send()
+
+    drain_sides(0)
+    drain_sides(1)
 
     def drain(index_of_parts, steps):
         def one(step, carry):
@@ -462,7 +506,7 @@
             pltpu.VMEM((2, HALF, FRAMES, SLOW), bf16),
             pltpu.VMEM((2, HALF, FRAMES, SLOW), bf16),
             dma((3,)),
-            dma((5,)),
+            dma((9,)),
             dma((CHUNKS, 2)),
             dma((CHUNKS, 2, peers)),
             dma((CHUNKS, 2, peers)),

time: 111 us -> 110 us (level)
    pallas_call x1, Pallas kernels: 110 us -> 109 us  [body(): pl.pallas_call(kernel, out_shape=pltpu.VMEM((2, BINS, FRAMES, SLOW), f32)...]
where the time goes in v5:
time: 110 us
  Pallas kernels  109 us (99%)
  local copies, waits for them, and re-layouts  1.32 us (1%)
    pallas_call x1, Pallas kernels, body(): pl.pallas_call(kernel, out_shape=pltpu.VMEM((2, BINS, FRAMES, SLOW), f32)...  109 us

profile of v5, /device:TPU:1, one launch (start us, length us, event | category | flops | bytes accessed | tf_op | source)
XLA Modules:
  0.0 110.0 jit_solution(17047717082656003707)
XLA Ops:
  0.0 108.7 %shard_map.46 = f32[2,16,128,128]{3,2,1,0:T(8,128)S(1)} custom-call(bf16[16,512,512]{2,1,0:T(8,128)(2,1)} %bitcast.2, f32[16,512]{1,0:T(8,128)} %taps_ref.1, bf16[256,512]{1,0:T(8,128)(2,1)} %constant.2.clone.fourier_ref, bf16[16,256,1024]{2,1,0:T(8,128)(2,1)} %bitcast.3), custom_call_target="tpu_custom_call" | custom-call | flops 12999999488 | bytes 20971520 | tf_op jit(solution)/shard_map/pallas_call | solution.py:489
  108.7 1.3 %copy.6 = f32[2,16,128,128]{3,2,1,0:T(8,128)} copy(f32[2,16,128,128]{3,2,1,0:T(8,128)S(1)} %shard_map.46) | data formatting | bytes 4194304

commit v6 on v5

--- a/solution.py
+++ b/solution.py
@@ -211,14 +211,15 @@
             device_id_type=MESH,
         )
 
-    back_copy = pltpu.make_async_remote_copy(
-        src_ref=back_out,
-        dst_ref=back_in,
-        send_sem=back_sem.at[0],
-        recv_sem=back_sem.at[1],
-        device_id=there(flipped, fibre),
-        device_id_type=MESH,
-    )
+    def back_copy(aperture):
+        return pltpu.make_async_remote_copy(
+            src_ref=back_out.at[aperture],
+            dst_ref=back_in.at[aperture],
+            send_sem=back_sem.at[0, aperture],
+            recv_sem=back_sem.at[1, aperture],
+            device_id=there(flipped, fibre),
+            device_id_type=MESH,
+        )
 
     parts = [jnp.where(hi == h, 0, 1) for h in range(2)]
     targets = [[jnp.where(hi == h, t, t + 1 - 2 * (t % 2)) for h in range(2)] for t in range(TM)]
@@ -422,13 +423,14 @@
     own(1)
     wait_sides(1)
 
-    def finish_other(k, carry):
-        for aperture in range(2):
+    for aperture in range(2):
+
+        def finish_other(k, carry):
             back_out[aperture, k] = power(1, aperture, k).astype(bf16)
-        return carry
-
-    lax.fori_loop(0, HALF, finish_other, 0)
-    back_copy.start()
+            return carry
+
+        lax.fori_loop(0, HALF, finish_other, 0)
+        back_copy(aperture).start()
 
     arrive(3, 0)
     combine(3, 0)
@@ -443,14 +445,14 @@
 
     lax.fori_loop(0, HALF, finish_own, 0)
 
-    back_copy.wait()
-
-    def place(k, carry):
-        for aperture in range(2):
+    for aperture in range(2):
+        back_copy(aperture).wait()
+
+        def place(k, carry):
             out_ref[aperture, (1 - hi) * HALF + k] = back_in[aperture, k].astype(f32)
-        return carry
-
-    lax.fori_loop(0, HALF, place, 0)
+            return carry
+
+        lax.fori_loop(0, HALF, place, 0)
 
     steer_swap.wait_send()
     steer_beside(odd_x).wait_send()
@@ -514,7 +516,7 @@
             dma((2, 2)),
             dma((2, 2)),
             dma((2, 2)),
-            dma((2,)),
+            dma((2, 2)),
         ],
         compiler_params=pltpu.CompilerParams(
             collective_id=0, has_side_effects=True, vmem_limit_bytes=60 * 2**20

time: 110 us -> 110 us (level)
  no operation moved by 1% of the time
where the time goes in v6:
time: 110 us
  Pallas kernels  109 us (99%)
  local copies, waits for them, and re-layouts  1.32 us (1%)
    pallas_call x1, Pallas kernels, body(): pl.pallas_call(kernel, out_shape=pltpu.VMEM((2, BINS, FRAMES, SLOW), f32)...  109 us

profile of v6, /device:TPU:1, one launch (start us, length us, event | category | flops | bytes accessed | tf_op | source)
XLA Modules:
  0.0 110.2 jit_solution(17974938709405647731)
XLA Ops:
  0.0 108.8 %shard_map.46 = f32[2,16,128,128]{3,2,1,0:T(8,128)S(1)} custom-call(bf16[16,512,512]{2,1,0:T(8,128)(2,1)} %bitcast.2, f32[16,512]{1,0:T(8,128)} %taps_ref.1, bf16[256,512]{1,0:T(8,128)(2,1)} %constant.2.clone.fourier_ref, bf16[16,256,1024]{2,1,0:T(8,128)(2,1)} %bitcast.3), custom_call_target="tpu_custom_call" | custom-call | flops 12999999488 | bytes 20971520 | tf_op jit(solution)/shard_map/pallas_call | solution.py:491
  108.8 1.3 %copy.6 = f32[2,16,128,128]{3,2,1,0:T(8,128)} copy(f32[2,16,128,128]{3,2,1,0:T(8,128)S(1)} %shard_map.46) | data formatting | bytes 4194304

commit v7 on v5

--- a/solution.py
+++ b/solution.py
@@ -29,8 +29,8 @@
 f32 = jnp.float32
 bf16 = jnp.bfloat16
 
-OFFSETS = ((2, 1), (0, 1), (2, 0), (1, 1), (1, 0), (3, 1), (3, 0))
-OFFSETS1 = ((3, 0), (3, 1), (1, 0), (1, 1), (2, 0), (0, 1), (2, 1))
+OFFSETS = ((2, 1), (0, 1), (1, 1), (2, 0), (1, 0), (3, 1), (3, 0))
+OFFSETS1 = ((3, 0), (3, 1), (1, 0), (2, 0), (1, 1), (0, 1), (2, 1))
 
 
 def dft_table():

time: 110 us -> 110 us (level)
  no operation moved by 1% of the time
where the time goes in v7:
time: 110 us
  Pallas kernels  108 us (98%)
  local copies, waits for them, and re-layouts  1.32 us (1%)
    pallas_call x1, Pallas kernels, body(): pl.pallas_call(kernel, out_shape=pltpu.VMEM((2, BINS, FRAMES, SLOW), f32)...  108 us

profile of v7, /device:TPU:1, one launch (start us, length us, event | category | flops | bytes accessed | tf_op | source)
XLA Modules:
  0.0 109.6 jit_solution(18140708138226132299)
XLA Ops:
  0.0 108.3 %shard_map.46 = f32[2,16,128,128]{3,2,1,0:T(8,128)S(1)} custom-call(bf16[16,512,512]{2,1,0:T(8,128)(2,1)} %bitcast.2, f32[16,512]{1,0:T(8,128)} %taps_ref.1, bf16[256,512]{1,0:T(8,128)(2,1)} %constant.2.clone.fourier_ref, bf16[16,256,1024]{2,1,0:T(8,128)(2,1)} %bitcast.3), custom_call_target="tpu_custom_call" | custom-call | flops 12999999488 | bytes 20971520 | tf_op jit(solution)/shard_map/pallas_call | solution.py:489
  108.3 1.3 %copy.6 = f32[2,16,128,128]{3,2,1,0:T(8,128)} copy(f32[2,16,128,128]{3,2,1,0:T(8,128)S(1)} %shard_map.46) | data formatting | bytes 4194304
